TPU v7x, 32 devices: a whole 2x2x4 slice. The times are simulated.
32 devices in a mesh: dp: 32 (over z, y, x, core), tp: 1.
Axes of the slice: x: 2, y: 2, z: 4, core: 2. Of those that a mesh axis runs over, the one named last changes fastest.
Arguments:
- hidden: bfloat16 [1024, 4, 5120], P('dp', None, 'tp'), may hold values from -6 to 6
- norm_gain: bfloat16 [5120], P('tp'), may hold values from 0.3984375 to 2.5
- w_query: bfloat16 [5120, 4096], P(None, 'tp'), may hold values from -0.078125 to 0.078125
- key_projection: bfloat16 [5120, 1024], P(None, 'tp'), may hold values from -0.078125 to 0.078125
- value_projection: bfloat16 [5120, 1024], P(None, 'tp'), may hold values from -0.078125 to 0.078125
- query_gain: bfloat16 [128], replicated, may hold values from 0.5 to 2
- key_gain: bfloat16 [128], replicated, may hold values from 0.5 to 2
- cache_keys: bfloat16 [32, 32, 2, 128, 1024], P('dp', None, None, None, 'tp'), may hold values from -400 to 400
- cached_value_pages: bfloat16 [32, 32, 2, 128, 1024], P('dp', None, None, None, 'tp'), may hold values from -6 to 6
- cache_len: int32 [1024], replicated, may hold values from 1 to 256, as said below
- remaining: int32 [1024], P('dp'), may hold values from 0 to 7
- page_row: int32 [32, 32, 2], replicated, may hold values from 0 to 32, as said below
- page_seq: int32 [32, 32, 2], replicated, may hold values from 0 to 1, as said below
Outputs:
- attention: bfloat16 [1024, 4, 4096], P('dp', None, 'tp')
- new_keys: bfloat16 [1024, 4, 1024], P('dp', None, 'tp')
- new_values: bfloat16 [1024, 4, 1024], P('dp', None, 'tp')
Inputs may be any that keep to these rules, and one draw needn't show every extreme that they name: `cache_len`: the pages of a row of n cached tokens fill exactly ceil(n / 128) slots. `page_row`: for holder group g, owner group o and slot c: the owner's row whose page the slot holds, or 32 for an empty slot. `page_seq`: each page number 0 to ceil(n / 128) - 1 of a row of n cached tokens appears once among the row's slots; empty slots hold 0.
All inputs are finite; a program needn't handle non-finite values.
Results may differ from a plain program's by a relative error of at most 0.015.
The roundings to bfloat16 on the way count: a program that leaves them out, or rounds other values in their place, can miss the bound.
Values may be sent and summed in bfloat16 or wider, within the bound.
A program may use at most 256 MiB of HBM per device.

v0:
```python
import math

import jax
import jax.numpy as jnp
from jax import lax
from jax.sharding import PartitionSpec as P

EPSILON = 1e-06
ROPE_BASE = 1000000.0
MASKED_SCORE = -1e30


def head_norm_rope(heads, gain_vector, positions):
    head_width = heads.shape[-1]
    half_width = head_width // 2
    scaled = (
        heads
        * lax.rsqrt(jnp.mean(heads * heads, axis=-1, keepdims=True) + EPSILON)
        * gain_vector.astype(jnp.float32)
    )
    frequency = jnp.exp(
        jnp.arange(half_width, dtype=jnp.float32) * (-2.0 * math.log(ROPE_BASE) / head_width)
    )
    angles = positions.astype(jnp.float32)[:, :, None, None] * frequency
    cosine = jnp.cos(angles)
    sine_part = jnp.sin(angles)
    first_half = scaled[..., :half_width]
    second = scaled[..., half_width:]
    return jnp.concatenate(
        [first_half * cosine - second * sine_part, second * cosine + first_half * sine_part],
        axis=-1,
    )


def masked_parts(group_scores, usable):
    group_scores = jnp.where(usable, group_scores, MASKED_SCORE)
    block_max = jnp.max(group_scores, axis=-1)
    weights = jnp.where(usable, jnp.exp(group_scores - block_max[..., None]), 0.0).astype(
        jnp.bfloat16
    )
    return (block_max, weights, jnp.sum(weights.astype(jnp.float32), axis=-1))


def page_partial(queries, page_keys, page_values, usable):
    scale = 1.0 / math.sqrt(queries.shape[-1])
    group_scores = (
        jnp.einsum("nkqd,npkd->nkqp", queries, page_keys, preferred_element_type=jnp.float32)
        * scale
    )
    block_max, weights, block_total = masked_parts(group_scores, usable[:, None, None, :])
    output = jnp.einsum("nkqp,npkd->nkqd", weights, page_values, preferred_element_type=jnp.float32)
    return (block_max, block_total, output)


def new_partial(arranged, fresh_keys, fresh_values, step_count):
    scale = 1.0 / math.sqrt(arranged.shape[-1])
    group_scores = (
        jnp.einsum("rkqd,rjkd->rkqj", arranged, fresh_keys, preferred_element_type=jnp.float32)
        * scale
    )
    step_index = jnp.arange(arranged.shape[2], dtype=jnp.int32) % step_count
    causal = jnp.arange(step_count, dtype=jnp.int32)[None, :] <= step_index[:, None]
    block_max, weights, block_total = masked_parts(group_scores, causal[None, None])
    output = jnp.einsum(
        "rkqj,rjkd->rkqd", weights, fresh_values, preferred_element_type=jnp.float32
    )
    return (block_max, block_total, output)


def combine_pages(
    page_rows, page_max, page_total, page_out, new_max, new_total, new_out, row_count
):
    row_hit = (page_rows[:, None] == jnp.arange(row_count, dtype=jnp.int32)[None, :])[
        :, :, None, None
    ]
    page_top = jnp.max(jnp.where(row_hit, page_max[:, None], MASKED_SCORE), axis=0)
    row_max = jnp.maximum(page_top, new_max)
    factor = jnp.exp(jnp.where(row_hit, page_max[:, None] - row_max[None], MASKED_SCORE))
    own_factor = jnp.exp(new_max - row_max)
    denominator = (
        jnp.einsum("nrkq,nkq->rkq", factor, page_total, precision=lax.Precision.HIGHEST)
        + own_factor * new_total
    )
    numerator = (
        jnp.einsum("nrkq,nkqd->rkqd", factor, page_out, precision=lax.Precision.HIGHEST)
        + own_factor[..., None] * new_out
    )
    return numerator / denominator[..., None]


def shards(
    hidden,
    norm_gain,
    w_query,
    key_projection,
    value_projection,
    query_gain,
    key_gain,
    cache_keys,
    cached_value_pages,
    cache_len,
    remaining,
    page_row,
    page_seq,
):
    gathered, full_gain = (
        lax.all_gather(hidden, "tp", axis=2, tiled=True),
        lax.all_gather(norm_gain, "tp", axis=0, tiled=True),
    )
    row_count, step_count, feature_count = gathered.shape
    head_width = query_gain.shape[0]
    groups = page_row.shape[0]
    capacity = page_row.shape[2]
    page_len = cache_keys.shape[3]
    kv_heads = key_projection.shape[1] // head_width
    my_group = lax.axis_index("dp")
    hidden_wide = gathered.astype(jnp.float32)
    normed = (
        hidden_wide
        * lax.rsqrt(jnp.mean(hidden_wide * hidden_wide, axis=-1, keepdims=True) + EPSILON)
        * full_gain.astype(jnp.float32)
    ).astype(jnp.bfloat16)
    flattened = normed.reshape(row_count * step_count, feature_count)
    local_lengths = lax.dynamic_slice_in_dim(cache_len, my_group * row_count, row_count)
    positions = local_lengths[:, None] + jnp.arange(step_count, dtype=jnp.int32)[None, :]
    queries = jnp.dot(flattened, w_query, preferred_element_type=jnp.float32).reshape(
        row_count, step_count, -1, head_width
    )
    queries = head_norm_rope(queries, query_gain, positions).astype(jnp.bfloat16)
    fresh_keys = jnp.dot(flattened, key_projection, preferred_element_type=jnp.float32).reshape(
        row_count, step_count, kv_heads, head_width
    )
    fresh_keys = head_norm_rope(fresh_keys, key_gain, positions).astype(jnp.bfloat16)
    fresh_values = (
        jnp.dot(flattened, value_projection, preferred_element_type=jnp.float32)
        .astype(jnp.bfloat16)
        .reshape(row_count, step_count, kv_heads, head_width)
    )
    group_size = queries.shape[2] // kv_heads
    arranged = (
        queries.reshape(row_count, step_count, kv_heads, group_size, head_width)
        .transpose(0, 2, 3, 1, 4)
        .reshape(row_count, kv_heads, group_size * step_count, head_width)
    )
    new_max, new_total, new_out = new_partial(arranged, fresh_keys, fresh_values, step_count)
    slot_count = groups * capacity
    token_index = jnp.arange(page_len, dtype=jnp.int32)[None, :]
    rows_sent = lax.dynamic_index_in_dim(page_row, my_group, 1, keepdims=False)
    page_rows = rows_sent.reshape(-1)
    got_keys, got_values = (
        lax.all_to_all(cache_keys, "dp", split_axis=1, concat_axis=0, tiled=True),
        lax.all_to_all(cached_value_pages, "dp", split_axis=1, concat_axis=0, tiled=True),
    )
    seq_sent = lax.dynamic_index_in_dim(page_seq, my_group, 1, keepdims=False).reshape(-1)
    safe_row = jnp.minimum(page_rows, row_count - 1)
    length_cap = jnp.where(page_rows < row_count, local_lengths[safe_row], 0)
    usable = seq_sent[:, None] * page_len + token_index < length_cap[:, None]
    page_max, page_total, page_out = page_partial(
        arranged[safe_row],
        got_keys.reshape(slot_count, page_len, kv_heads, head_width),
        got_values.reshape(slot_count, page_len, kv_heads, head_width),
        usable,
    )
    attended = combine_pages(
        page_rows, page_max, page_total, page_out, new_max, new_total, new_out, row_count
    )
    attended = (
        attended.reshape(row_count, kv_heads, group_size, step_count, head_width)
        .transpose(0, 3, 1, 2, 4)
        .reshape(row_count, step_count, -1)
    )
    live = jnp.arange(step_count, dtype=jnp.int32)[None, :] < remaining[:, None]
    attention = jnp.where(live[:, :, None], attended, 0.0).astype(jnp.bfloat16)
    return (
        attention,
        fresh_keys.reshape(row_count, step_count, -1),
        fresh_values.reshape(row_count, step_count, -1),
    )


def solution(mesh):
    in_specs = (
        P("dp", None, "tp"),
        P("tp"),
        P(None, "tp"),
        P(None, "tp"),
        P(None, "tp"),
        P(),
        P(),
        P("dp", None, None, None, "tp"),
        P("dp", None, None, None, "tp"),
        P(),
        P("dp"),
        P(),
        P(),
    )
    out_specs = (P("dp", None, "tp"), P("dp", None, "tp"), P("dp", None, "tp"))
    return jax.shard_map(shards, mesh=mesh, in_specs=in_specs, out_specs=out_specs, check_vma=False)
```

profile of v0, /device:TPU:0, one launch (start us, length us, event | category | flops | bytes accessed | tf_op | source)
XLA Modules:
  0.0 824.2 jit_solution(11397427246755559624)
XLA Ops:
  0.6 22.5 %copy.130 = bf16[1,32,2,128,1024]{3,4,2,0,1:T(8,128)(2,1)} copy(bf16[1,32,2,128,1024]{4,3,2,1,0:T(8,128)(2,1)} %param.20) | data formatting | bytes 33554432 | tf_op args[7]
  23.2 370.7 %all_to_all.8 = bf16[1,32,2,128,1024]{3,4,2,0,1:T(8,128)(2,1)} all-to-all(bf16[1,32,2,128,1024]{3,4,2,0,1:T(8,128)(2,1)} %copy.130), channel_id=1, replica_groups=mesh['dp'=32,'tp'=1] {'dp'}, dimensions={1} | all-to-all | bytes 33554432 | tf_op jit(solution)/shard_map/all_to_all | solution.py:151
  393.9 4.3 all-to-all-start.1
  398.3 0.0 copy-start.6
  398.3 0.0 copy-start.16
  398.3 0.0 copy-start
  398.3 55.4 %copy.156 = bf16[4096,5120]{1,0:T(8,128)(2,1)} copy(bf16[4096,5120]{0,1:T(8,128)(2,1)} %bitcast.49) | data formatting | bytes 83886080 | tf_op jit(solution)/shard_map/dot_general | solution.py:126
  453.7 0.0 copy-done.16
  453.7 0.8 dynamic_slice.12
  454.5 0.0 copy-done
  454.5 0.8 fusion.3
  455.3 0.0 copy-done.6
  455.3 0.7 fusion.40
  456.0 21.2 %multiply_reduce_fusion = (f32[32,4,32]{0,2,1:T(8,128)S(1)}, f32[32,4,32,128]{3,0,2,1:T(8,128)}) fusion(bf16[32,128,5120,1]{2,1,0,3:T(8,128)(2,1)} %bitcast.50, bf16[32,4,5120,1]{2,1,0,3:T(4,128)(2,1)S(1)} %fusion.40), kind=kOutput, calls=%fused_computation.23 | convolution fusion | flops 5369753600 | bytes 45367296 | tf_op jit(solution)/shard_map/dot_general | solution.py:126
  477.2 0.0 copy-done.3
  477.3 0.3 multiply_cosine_fusion
  477.6 1.9 multiply_multiply_fusion
  479.5 0.8 subtract_convert_fusion
  480.3 0.0 copy-start.7
  480.3 0.0 copy-start.8
  480.3 0.6 maximum_bitcast_fusion
  480.9 1.8 copy.129
  482.7 2.4 dynamic-slice_reduce_fusion
  485.1 0.1 min.18
  485.2 1.3 gather_fusion
  486.5 2.3 gather_fusion.1
  488.8 1.4 reshape.277
  490.2 1.3 mul.191
  491.5 13.7 %copy.159 = bf16[1024,5120]{1,0:T(8,128)(2,1)} copy(bf16[1024,5120]{0,1:T(8,128)(2,1)} %bitcast.52) | data formatting | bytes 20971520 | tf_op jit(solution)/shard_map/dot_general | solution.py:130
  505.3 0.7 convert_element_type.56
  505.9 7.1 multiply_reduce_fusion.1
  513.0 0.0 copy-start.1
  513.0 0.2 multiply_multiply_fusion.1
  513.2 0.2 multiply_subtract_fusion
  513.5 0.1 maximum_convert_fusion
  513.7 0.8 copy.160
  514.5 1.5 fusion.30
  516.0 0.7 copy.139
  516.7 2.2 convert_reduce_fusion.1
  518.9 1.6 copy.144
  520.5 2.5 fusion.5
  523.0 2.5 reshape.281
  525.5 0.0 copy-start.15
  525.5 6.2 convolution_convert_fusion
  531.8 1.8 reshape_reshape.3
  533.5 1.0 copy.162
  534.5 1.7 reshape.307
  536.2 0.6 compare_select_fusion.1
  536.8 0.1 iota_compare_fusion.1
  536.9 0.1 add_compare_fusion
  537.0 3.0 fusion.23
  540.0 9.4 %fusion.2 = (f32[64,8,16]{2,1,0:T(8,128)S(1)}, f32[64,8,16,128]{3,2,1,0:T(8,128)}) fusion(pred[64,128]{1,0:T(8,128)(4,1)S(1)} %add_compare_fusion, bf16[64,8,16,128]{3,2,1,0:T(8,128)(2,1)S(1)} %gather_fusion.1, bf16[64,128,8,128]{1,3,2,0:T(8,128)(2,1)} %bitcast.47), kind=kOutput, calls=%fused_computation.7 | convolution fusion | flops 271572992 | bytes 23109632 | tf_op jit(solution)/shard_map/nkqd,npkd->nkqp/dot_general | solution.py:47
  549.4 0.1 copy.135
  549.6 4.5 convert_reduce_fusion
  554.1 216.9 %all-to-all-done.1 = bf16[1,32,2,128,1024]{4,3,2,0,1:T(8,128)(2,1)} async-done(((bf16[1,32,2,128,1024]{4,3,2,0,1:T(8,128)(2,1)}), bf16[1,32,2,128,1024]{4,3,2,0,1:T(8,128)(2,1)}, u32[]{:S(2)}, u32[]{:S(2)}) %all-to-all-start.1) | async-done | bytes 16777248 | tf_op jit(solution)/shard_map/all_to_all | solution.py:152
  770.9 22.5 %copy.133 = bf16[1,32,2,128,1024]{3,4,2,1,0:T(8,128)(2,1)} copy(bf16[1,32,2,128,1024]{4,3,2,0,1:T(8,128)(2,1)} %all-to-all-done.1) | data formatting | bytes 33554432 | tf_op jit(solution)/shard_map/all_to_all | solution.py:152
  793.5 14.4 %fusion.29 = f32[64,8,16,128]{3,2,1,0:T(8,128)} fusion(bf16[64,128,8,128]{1,3,2,0:T(8,128)(2,1)} %bitcast.48, f32[64,8,16,128]{3,2,1,0:T(8,128)} %get-tuple-element.38, f32[64,8,16]{2,1,0:T(8,128)S(1)} %get-tuple-element.37, pred[64,128]{1,0:T(8,128)(4,1)S(1)} %add_compare_fusion), kind=kOutput, calls=%fused_computation.73 | convolution fusion | flops 273678336 | bytes 25206784 | tf_op jit(solution)/shard_map/nkqp,npkd->nkqd/dot_general | solution.py:51
  807.9 0.1 copy.152
  808.0 0.6 select_reduce_fusion
  808.6 3.5 fusion.7
  812.2 9.2 %fusion.6 = bf16[32,8,16,128]{3,0,2,1:T(8,128)(2,1)S(1)} fusion(f32[32,8,16,128]{3,2,1,0:T(8,128)S(1)} %copy-done.2, f32[32,8,16]{0,2,1:T(8,128)S(1)} %get-tuple-element.23, f32[32,8,16]{0,2,1:T(8,128)S(1)} %get-tuple-element.24, f32[32,8,16]{0,2,1:T(8,128)S(1)} %max.11, f32[64,8,16]{0,2,1:T(8,128)S(1)} %copy.135, pred[64,32]{0,1:T(8,128)(4,1)S(1)} %iota_compare_fusion, ...), kind=kOutput, calls=%fused_computation.14 | convolution fusion | flops 405274624 | bytes 7424000 | tf_op jit(solution)/shard_map/nrkq,nkqd->rkqd/dot_general | solution.py:85
  821.4 0.8 copy.145
  822.2 0.3 reshape.284
  822.5 1.6 select_convert_fusion.1
  (37 shorter events, 0.2 us)
Async XLA Ops:
  393.9 4.4 copy-start.9
  393.9 377.0 %all-to-all-start.1 = ((bf16[1,32,2,128,1024]{4,3,2,0,1:T(8,128)(2,1)}), bf16[1,32,2,128,1024]{4,3,2,0,1:T(8,128)(2,1)}, u32[]{:S(2)}, u32[]{:S(2)}) async-start(bf16[1,32,2,128,1024]{4,3,2,0,1:T(8,128)(2,1)} %bitcast.51), calls=%async_computation.1 | async-start | bytes 33554432 | tf_op jit(solution)/shard_map/all_to_all | solution.py:152
  398.3 57.0 %copy-start.6 = (f32[5120]{0:T(1024)}, f32[5120]{0:T(1024)S(1)}, u32[]{:S(2)}) copy-start(f32[5120]{0:T(1024)S(1)} %convert_element_type.51) | copy-start | bytes 61444
  398.3 55.4 %copy-start.16 = (bf16[128]{0:T(256)(128)(2,1)S(1)}, bf16[128]{0:T(256)(128)(2,1)}, u32[]{:S(2)}) copy-start(bf16[128]{0:T(256)(128)(2,1)} %param.18) | copy-start | bytes 772
  398.3 56.2 %copy-start = (bf16[32,4,5120]{2,1,0:T(4,128)(2,1)S(1)}, bf16[32,4,5120]{2,1,0:T(4,128)(2,1)}, u32[]{:S(2)}) copy-start(bf16[32,4,5120]{2,1,0:T(4,128)(2,1)} %param.13) | copy-start | bytes 3932164
  456.0 21.2 %copy-start.3 = (bf16[32,4,5120,1]{2,1,0,3:T(4,128)(2,1)}, bf16[32,4,5120,1]{2,1,0,3:T(4,128)(2,1)S(1)}, u32[]{:S(2)}) copy-start(bf16[32,4,5120,1]{2,1,0,3:T(4,128)(2,1)S(1)} %fusion.40) | copy-start | bytes 3932164
  480.3 2.4 copy-start.7
  480.3 2.4 copy-start.8
  485.2 1.3 copy-start.10
  513.0 1.5 copy-start.1
  514.5 1.5 copy-start.13
  525.5 10.7 %copy-start.11 = (s32[64]{0:T(128)S(1)}, s32[64]{0:T(128)}, u32[]{:S(2)}) copy-start(s32[64]{0:T(128)} %reshape.277) | copy-start | bytes 772
  525.5 11.3 %copy-start.15 = (s32[32]{0:T(128)S(1)}, s32[32]{0:T(128)}, u32[]{:S(2)}) copy-start(s32[32]{0:T(128)} %param.23) | copy-start | bytes 388
  525.5 11.4 %copy-start.12 = (s32[64]{0:T(128)S(1)}, s32[64]{0:T(128)}, u32[]{:S(2)}) copy-start(s32[64]{0:T(128)} %mul.191) | copy-start | bytes 772
  525.5 11.5 %copy-start.14 = (pred[16,4]{0,1:T(4,128)(4,1)S(1)}, pred[16,4]{0,1:T(4,128)(4,1)}, u32[]{:S(2)}) copy-start(pred[16,4]{0,1:T(4,128)(4,1)} %copy-done.13) | copy-start | bytes 196
  793.5 15.2 %copy-start.4 = (f32[32,8,16]{0,2,1:T(8,128)S(1)}, f32[32,8,16]{0,2,1:T(8,128)}, u32[]{:S(2)}) copy-start(f32[32,8,16]{0,2,1:T(8,128)} %copy.139) | copy-start | bytes 49156
  807.9 4.3 copy-start.5
  807.9 4.3 copy-start.2
where the time goes:
time: 828 us; the launch traced here: 824 us
  blocking collectives  371 us (45%)
  waiting for transfers between devices  217 us (26%)
  local copies, waits for them, and re-layouts  135 us (16%)
  matrix products  75.5 us (9%)
  other arithmetic  21.1 us (3%)
    all_to_all x1, blocking collectives, shards(): lax.all_to_all(cache_keys, 'dp', split_axis=1, concat_axis=0, tiled=True)  371 us
    all_to_all x1, waiting for transfers between devices, shards(): lax.all_to_all(cached_value_pages, 'dp', split_axis=1, concat_axis=0, til...  217 us
    dot_general x1, local copies, waits for them, and re-layouts, shards(): jnp.dot(flattened, w_query, preferred_element_type=jnp.float32)  55.4 us
    unnamed x38, local copies, waits for them, and re-layouts  26.2 us
    all_to_all x1, local copies, waits for them, and re-layouts, shards(): lax.all_to_all(cached_value_pages, 'dp', split_axis=1, concat_axis=0, til...  22.5 us
    dot_general x1, matrix products, shards(): jnp.dot(flattened, w_query, preferred_element_type=jnp.float32)  21.2 us
  transfers between devices with their start and end apart: 1, of which 1 were waited for; matrix products, arithmetic and copies ran while one was open for 19% of the time, Pallas kernels for 0%

commit v1 on v0

v1 whole, which is shorter than its diff:
```python
import functools
import math

import jax
import jax.numpy as jnp
from jax import lax
from jax.experimental import pallas as pl
from jax.experimental.pallas import tpu as pltpu
from jax.sharding import PartitionSpec as P

EPSILON = 1e-06
ROPE_BASE = 1000000.0
MASKED_SCORE = -1e30
DEPTH = 4
WEIGHT_BUFFERS = 3


def soft_parts(scores, mask, head_width):
    scores = jnp.where(mask, scores * (1.0 / math.sqrt(head_width)), MASKED_SCORE)
    top = jnp.max(scores, axis=0, keepdims=True)
    weights = jnp.where(mask, jnp.exp(scores - top), 0.0)
    weights = weights.astype(jnp.bfloat16).astype(jnp.float32)
    return top, jnp.sum(weights, axis=0, keepdims=True), weights.T.astype(jnp.bfloat16)


def spread_dot(keys, block_q):
    return lax.dot_general(
        keys, block_q, (((1,), (1,)), ((), ())), preferred_element_type=jnp.float32
    )


def exchange_kernel(
    n,
    sizes,
    row_ref,
    seq_ref,
    len_ref,
    slot_ref,
    x_ref,
    gain_ref,
    cos_ref,
    sin_ref,
    q_gain_ref,
    k_gain_ref,
    wq_ref,
    wk_ref,
    wv_ref,
    ck_ref,
    cv_ref,
    out_ref,
    nk_ref,
    nv_ref,
    normed,
    wbuf,
    q_own,
    q_send,
    q_recv,
    o_send,
    o_recv,
    s_send,
    s_recv,
    kbuf,
    vbuf,
    block_q,
    new_o,
    new_s,
    q_ssem,
    q_rsem,
    o_ssem,
    o_rsem,
    s_ssem,
    s_rsem,
    ksem,
    vsem,
    wsem,
):
    rows, heads, per_head, head_width, steps, cap, page, depth, parts = sizes
    width = heads * per_head
    part_heads = heads // parts
    part_rows = part_heads * per_head
    block_cols = wbuf.shape[2]
    key_cols = min(block_cols, wk_ref.shape[1])
    key_blocks = wk_ref.shape[1] // key_cols
    blocks = heads + 2 * key_blocks
    bufs = wbuf.shape[0]
    me = lax.axis_index("dp")

    def distance(k):
        return k // 2 + (n // 2) * lax.rem(k, 2)

    def after(k):
        return lax.rem(me + distance(k), n)

    def before(k):
        return lax.rem(me + n - distance(k), n)

    def own_row(holder, c):
        return jnp.minimum(row_ref[(holder * n + me) * cap + c], rows - 1)

    def usable_tokens(owner, c):
        index = (me * n + owner) * cap + c
        row = row_ref[index]
        length = len_ref[owner * rows + jnp.minimum(row, rows - 1)]
        return jnp.where(row < rows, length, 0) - seq_ref[index] * page

    def fetch(k):
        owner, buf = before(k), lax.rem(k, depth)
        return (
            pltpu.make_async_copy(ck_ref.at[owner], kbuf.at[buf], ksem.at[buf]),
            pltpu.make_async_copy(cv_ref.at[owner], vbuf.at[buf], vsem.at[buf]),
        )

    def weight(j, act):
        buf = lax.rem(j, bufs)

        def move(ref, at, cols):
            src = ref.at[:, pl.ds(pl.multiple_of(at * cols, cols), cols)]
            dst = wbuf.at[buf, :, pl.ds(0, cols)]
            act(pltpu.make_async_copy(src, dst, wsem.at[buf]))

        @pl.when(j < heads)
        def _():
            move(wq_ref, j, block_cols)

        @pl.when((j >= heads) & (j < heads + key_blocks))
        def _():
            move(wk_ref, j - heads, key_cols)

        @pl.when((j >= heads + key_blocks) & (j < blocks))
        def _():
            move(wv_ref, j - heads - key_blocks, key_cols)

    def start(copy):
        copy.start()

    def wait(copy):
        copy.wait()

    def project(j, cols):
        weight(j + bufs - 1, start)
        weight(j, wait)
        return jnp.dot(
            normed[...],
            wbuf[lax.rem(j, bufs), :, 0:cols],
            preferred_element_type=jnp.float32,
        )

    def rotated(made, gain):
        done = []
        for h in range(made.shape[1] // head_width):
            y = made[:, h * head_width : (h + 1) * head_width]
            y = y * lax.rsqrt(jnp.mean(y * y, axis=-1, keepdims=True) + EPSILON) * gain
            done.append(y * cos_ref[...] + pltpu.roll(y, head_width // 2, 1) * sin_ref[...])
        return done

    def send_query(part, k):
        peer = after(k)
        return pltpu.make_async_remote_copy(
            src_ref=q_send.at[part, peer],
            dst_ref=q_recv.at[part, me],
            send_sem=q_ssem.at[part, peer],
            recv_sem=q_rsem.at[part, me],
            device_id={"dp": peer},
            device_id_type=pl.DeviceIdType.MESH,
        )

    def recv_query(part, k):
        owner = before(k)
        return pltpu.make_async_remote_copy(
            src_ref=q_send.at[part, owner],
            dst_ref=q_recv.at[part, owner],
            send_sem=q_ssem.at[part, owner],
            recv_sem=q_rsem.at[part, owner],
            device_id={"dp": owner},
            device_id_type=pl.DeviceIdType.MESH,
        )

    def send_back(owner, slot):
        to = dict(device_id={"dp": owner}, device_id_type=pl.DeviceIdType.MESH)
        return (
            pltpu.make_async_remote_copy(
                src_ref=o_send.at[owner],
                dst_ref=o_recv.at[slot],
                send_sem=o_ssem.at[owner],
                recv_sem=o_rsem.at[slot],
                **to,
            ),
            pltpu.make_async_remote_copy(
                src_ref=s_send.at[owner],
                dst_ref=s_recv.at[slot],
                send_sem=s_ssem.at[owner],
                recv_sem=s_rsem.at[slot],
                **to,
            ),
        )

    for j in range(bufs - 1):
        weight(jnp.int32(j), start)
    for k in range(depth - 1):
        for copy in fetch(k):
            copy.start()

    barrier = pltpu.get_barrier_semaphore()

    @pl.loop(1, n)
    def _(k):
        pl.semaphore_signal(
            barrier, inc=1, device_id={"dp": after(k)}, device_id_type=pl.DeviceIdType.MESH
        )

    block_q[...] = jnp.zeros_like(block_q)
    x = x_ref[...].astype(jnp.float32).reshape(normed.shape)
    scale = lax.rsqrt(jnp.mean(x * x, axis=-1, keepdims=True) + EPSILON)
    normed[...] = (x * scale * gain_ref[...].astype(jnp.float32)).astype(jnp.bfloat16)

    for part in range(parts):

        @pl.loop(part * part_heads, (part + 1) * part_heads)
        def _(h):
            done = rotated(project(h, block_cols), q_gain_ref[...].astype(jnp.float32))
            done = [y.reshape(rows, steps, head_width) for y in done]
            at = pl.ds(pl.multiple_of(h * per_head, per_head), per_head)
            q_own[:, at, :] = jnp.concatenate(done, axis=1).astype(jnp.bfloat16)

        if part == 0:
            pl.semaphore_wait(barrier, n - 1)
        span = slice(part * part_rows, (part + 1) * part_rows)

        @pl.loop(1, n)
        def _(k):
            peer = after(k)
            for c in range(cap):
                q_send[part, peer, c] = q_own[own_row(peer, c), span]
            send_query(part, k).start()

        for c in range(cap):
            q_recv[part, me, c] = q_own[own_row(me, c), span]

    @pl.loop(0, key_blocks)
    def _(j):
        done = rotated(project(j + heads, key_cols), k_gain_ref[...].astype(jnp.float32))
        at = pl.ds(pl.multiple_of(j * key_cols, key_cols), key_cols)
        nk_ref[:, at] = jnp.concatenate(done, axis=1).astype(jnp.bfloat16)

    @pl.loop(0, key_blocks)
    def _(j):
        at = pl.ds(pl.multiple_of(j * key_cols, key_cols), key_cols)
        nv_ref[:, at] = project(j + heads + key_blocks, key_cols).astype(jnp.bfloat16)

    position = lax.broadcasted_iota(jnp.int32, (page, width), 0)

    def columns(h):
        return slice(h * head_width, (h + 1) * head_width)

    def stripe(h):
        return slice(h * per_head, (h + 1) * per_head)

    @pl.loop(0, n)
    def _(k):
        owner, buf = before(k), lax.rem(k, depth)

        @pl.when(k + depth - 1 < n)
        def _():
            for copy in fetch(k + depth - 1):
                copy.start()

        @pl.when(k > 0)
        def _():
            for part in range(parts):
                recv_query(part, k).wait_recv()

        for copy in fetch(k):
            copy.wait()
        scores = []
        for c in range(cap):
            for h in range(heads):
                part, first = h // part_heads, (h % part_heads) * per_head
                block_q[c, stripe(h), columns(h)] = q_recv[
                    part, owner, c, first : first + per_head
                ]
            scores.append(spread_dot(kbuf[buf, c], block_q[c]))
        turned = []
        for c in range(cap):
            mask = position < usable_tokens(owner, c)
            top, total, weights = soft_parts(scores[c], mask, head_width)
            s_send[owner, 2 * c : 2 * c + 1, 0:width] = top
            s_send[owner, 2 * c + 1 : 2 * c + 2, 0:width] = total
            turned.append(weights)
        for c in range(cap):
            for h in range(heads):
                o_send[owner, c, stripe(h)] = jnp.dot(
                    turned[c][stripe(h)],
                    vbuf[buf, c, :, columns(h)],
                    preferred_element_type=jnp.float32,
                ).astype(jnp.bfloat16)

        @pl.when(k > 0)
        def _():
            for copy in send_back(owner, me):
                copy.start()

    per_tile = 16 // steps
    token = lax.broadcasted_iota(jnp.int32, (16, width), 0)
    step = lax.rem(lax.broadcasted_iota(jnp.int32, (16, width), 1), steps)
    masks = [(token >= i * steps) & (token <= i * steps + step) for i in range(per_tile)]

    @pl.loop(0, rows // per_tile)
    def _(tile):
        at = pl.ds(pl.multiple_of(tile * 16, 16), 16)
        keys, values = nk_ref[at], nv_ref[at]
        scores = []
        for i in range(per_tile):
            for h in range(heads):
                block_q[i, stripe(h), columns(h)] = q_own[tile * per_tile + i, stripe(h)]
            scores.append(spread_dot(keys, block_q[i]))
        turned = []
        for i in range(per_tile):
            row = tile * per_tile + i
            top, total, weights = soft_parts(scores[i], masks[i], head_width)
            new_s[row, 0:1, 0:width] = top
            new_s[row, 1:2, 0:width] = total
            turned.append(weights)
        for h in range(heads):
            stacked = jnp.concatenate([w[stripe(h)] for w in turned], axis=0)
            outs = jnp.dot(stacked, values[:, columns(h)], preferred_element_type=jnp.float32)
            for i in range(per_tile):
                new_o[tile * per_tile + i, stripe(h)] = outs[stripe(i)]

    o_recv[me] = o_send[me]
    s_recv[me] = s_send[me]

    @pl.loop(1, n)
    def _(k):
        for part in range(parts):
            send_query(part, k).wait_send()
        for copy in send_back(before(k), me):
            copy.wait_send()
        for copy in send_back(after(k), after(k)):
            copy.wait_recv()

    @pl.loop(0, rows, unroll=2)
    def _(r):
        first, second = slot_ref[r], slot_ref[rows + r]
        has_second = slot_ref[2 * rows + r]

        def stats(slot):
            both = s_recv[slot // cap]
            top, total = both[0:1], both[1:2]
            for c in range(1, cap):
                hit = lax.rem(slot, cap) == c
                top = jnp.where(hit, both[2 * c : 2 * c + 1], top)
                total = jnp.where(hit, both[2 * c + 1 : 2 * c + 2], total)
            return top, total

        top_a, total_a = stats(first)
        top_b, total_b = stats(second)
        top_b = jnp.where(has_second > 0, top_b, MASKED_SCORE)
        total_b = jnp.where(has_second > 0, total_b, 0.0)
        top_n, total_n = new_s[r, 0:1], new_s[r, 1:2]
        top = jnp.maximum(jnp.maximum(top_a, top_b), top_n)
        fa, fb, fn = jnp.exp(top_a - top), jnp.exp(top_b - top), jnp.exp(top_n - top)
        fb = jnp.where(has_second > 0, fb, 0.0)
        share = 1.0 / (fa * total_a + fb * total_b + fn * total_n)
        factors = jnp.concatenate(
            [fa * share, fb * share, fn * share, jnp.zeros((5, fa.shape[1]), jnp.float32)], axis=0
        ).T[0:width]
        out_a = o_recv[first // cap, lax.rem(first, cap)].astype(jnp.float32)
        out_b = o_recv[second // cap, lax.rem(second, cap)].astype(jnp.float32)
        out = factors[:, 0:1] * out_a + factors[:, 1:2] * out_b + factors[:, 2:3] * new_o[r]
        out_ref[r] = out.astype(out_ref.dtype)


def shards(
    hidden,
    norm_gain,
    w_query,
    key_projection,
    value_projection,
    query_gain,
    key_gain,
    cache_keys,
    cached_value_pages,
    cache_len,
    remaining,
    page_row,
    page_seq,
):
    gathered, full_gain = (
        lax.all_gather(hidden, "tp", axis=2, tiled=True),
        lax.all_gather(norm_gain, "tp", axis=0, tiled=True),
    )
    row_count, step_count, feature_count = gathered.shape
    head_width = query_gain.shape[0]
    groups = page_row.shape[0]
    capacity = page_row.shape[2]
    page_len = cache_keys.shape[3]
    kv_heads = key_projection.shape[1] // head_width
    my_group = lax.axis_index("dp")
    tokens = row_count * step_count
    local_lengths = lax.dynamic_slice_in_dim(cache_len, my_group * row_count, row_count)
    positions = local_lengths[:, None] + jnp.arange(step_count, dtype=jnp.int32)[None, :]
    half = head_width // 2
    frequency = jnp.exp(
        jnp.arange(half, dtype=jnp.float32) * (-2.0 * math.log(ROPE_BASE) / head_width)
    )
    angles = positions.astype(jnp.float32).reshape(tokens, 1) * frequency
    cosine, sine = jnp.cos(angles), jnp.sin(angles)
    cosine = jnp.concatenate([cosine, cosine], axis=1)
    sine = jnp.concatenate([-sine, sine], axis=1)
    query_heads = w_query.shape[1] // head_width
    group_size = query_heads // kv_heads
    per_head = group_size * step_count
    sent_rows = lax.dynamic_index_in_dim(page_row, my_group, 1, keepdims=False).reshape(-1)
    sent_seq = lax.dynamic_index_in_dim(page_seq, my_group, 1, keepdims=False).reshape(-1)
    row_index = jnp.arange(row_count, dtype=jnp.int32)[:, None]
    holds = sent_rows[None, :] == row_index
    slot_count = groups * capacity
    slot_index = jnp.arange(slot_count, dtype=jnp.int32)[None, :]
    shifted = slot_index * jnp.where(sent_seq == 0, 1, slot_count)[None, :]
    both = jnp.sum(jnp.where(holds, shifted, 0), axis=1)
    slot_a, slot_b = both % slot_count, both // slot_count
    has_b = (local_lengths > page_len).astype(jnp.int32)
    slots = jnp.concatenate([slot_a, slot_b, has_b])
    width = kv_heads * per_head
    lanes = max(128, width)
    sizes = (row_count, kv_heads, per_head, head_width, step_count, capacity, page_len)
    parts = 2 if kv_heads % 2 == 0 else 1
    sizes = sizes + (DEPTH, parts)
    smem = pl.BlockSpec(memory_space=pltpu.SMEM)
    vmem = pl.BlockSpec(memory_space=pltpu.VMEM)
    hbm = pl.BlockSpec(memory_space=pl.ANY)
    bf16, f32 = jnp.bfloat16, jnp.float32
    features = kv_heads * head_width
    dma = pltpu.SemaphoreType.DMA
    attended, fresh_keys, fresh_values = pl.pallas_call(
        functools.partial(exchange_kernel, groups, sizes),
        out_shape=(
            jax.ShapeDtypeStruct((row_count, width, head_width), bf16),
            jax.ShapeDtypeStruct((tokens, features), bf16),
            jax.ShapeDtypeStruct((tokens, features), bf16),
        ),
        in_specs=[smem] * 4 + [vmem] * 6 + [hbm] * 5,
        out_specs=(vmem, vmem, vmem),
        scratch_shapes=[
            pltpu.VMEM((tokens, feature_count), bf16),
            pltpu.VMEM((WEIGHT_BUFFERS, feature_count, group_size * head_width), bf16),
            pltpu.VMEM((row_count, width, head_width), bf16),
            pltpu.VMEM((parts, groups, capacity, width // parts, head_width), bf16),
            pltpu.VMEM((parts, groups, capacity, width // parts, head_width), bf16),
            pltpu.VMEM((groups, capacity, width, head_width), bf16),
            pltpu.VMEM((groups, capacity, width, head_width), bf16),
            pltpu.VMEM((groups, 2 * capacity, lanes), f32),
            pltpu.VMEM((groups, 2 * capacity, lanes), f32),
            pltpu.VMEM((DEPTH, capacity, page_len, features), bf16),
            pltpu.VMEM((DEPTH, capacity, page_len, features), bf16),
            pltpu.VMEM((max(capacity, 16 // step_count), width, features), bf16),
            pltpu.VMEM((row_count, width, head_width), f32),
            pltpu.VMEM((row_count, 2, lanes), f32),
        ]
        + [dma((parts, groups))] * 2
        + [dma((groups,))] * 4
        + [dma((DEPTH,))] * 2
        + [dma((WEIGHT_BUFFERS,))],
        compiler_params=pltpu.CompilerParams(
            collective_id=0, has_side_effects=True, vmem_limit_bytes=56 * 1024 * 1024
        ),
        name="page_exchange",
    )(
        page_row.reshape(-1),
        page_seq.reshape(-1),
        cache_len,
        slots,
        gathered,
        full_gain.reshape(1, feature_count),
        cosine,
        sine,
        query_gain.reshape(1, head_width),
        key_gain.reshape(1, head_width),
        w_query,
        key_projection,
        value_projection,
        cache_keys.reshape(groups, capacity, page_len, features),
        cached_value_pages.reshape(groups, capacity, page_len, features),
    )
    attended = (
        attended.reshape(row_count, kv_heads, group_size, step_count, head_width)
        .transpose(0, 3, 1, 2, 4)
        .reshape(row_count, step_count, -1)
    )
    live = jnp.arange(step_count, dtype=jnp.int32)[None, :] < remaining[:, None]
    attention = jnp.where(live[:, :, None], attended, 0.0).astype(jnp.bfloat16)
    return (
        attention,
        fresh_keys.reshape(row_count, step_count, -1),
        fresh_values.reshape(row_count, step_count, -1),
    )


def solution(mesh):
    in_specs = (
        P("dp", None, "tp"),
        P("tp"),
        P(None, "tp"),
        P(None, "tp"),
        P(None, "tp"),
        P(),
        P(),
        P("dp", None, None, None, "tp"),
        P("dp", None, None, None, "tp"),
        P(),
        P("dp"),
        P(),
        P(),
    )
    out_specs = (P("dp", None, "tp"), P("dp", None, "tp"), P("dp", None, "tp"))
    return jax.shard_map(shards, mesh=mesh, in_specs=in_specs, out_specs=out_specs, check_vma=False)
```

time: 828 us -> 135 us (0.16)
  blocking collectives: 371 us -> 0 us
  waiting for transfers between devices: 217 us -> 0 us
  local copies, waits for them, and re-layouts: 135 us -> 8.91 us
  Pallas kernels: 0 us -> 117 us
  matrix products: 75.5 us -> 0 us
  other arithmetic: 21.1 us -> 8.13 us
    all_to_all x1 -> x0, blocking collectives: 371 us -> none  [shards(): lax.all_to_all(cache_keys, 'dp', split_axis=1, concat_axis=0, tiled=True)]
    all_to_all x1 -> x0, waiting for transfers between devices: 217 us -> none  [shards(): lax.all_to_all(cached_value_pages, 'dp', split_axis=1, concat_axis=0, til...]
    pallas_call x0 -> x1, Pallas kernels: none -> 117 us  [shards(): pl.pallas_call(functools.partial(exchange_kernel, groups, sizes), out_sha...]
    dot_general x9 -> x0, matrix products: 75.5 us -> none  [the longest x1 21.2 us: shards(): jnp.dot(flattened, w_query, preferred_element_type=jnp.float32)]
    dot_general x2 -> x0, local copies, waits for them, and re-layouts: 69.1 us -> none  [the longest x1 55.4 us: shards(): jnp.dot(flattened, w_query, preferred_element_type=jnp.float32)]
    unnamed x38 -> x2, local copies, waits for them, and re-layouts: 26.2 us -> 2.04 us
    all_to_all x1 -> x0, local copies, waits for them, and re-layouts: 22.5 us -> none  [shards(): lax.all_to_all(cached_value_pages, 'dp', split_axis=1, concat_axis=0, til...]
  transfers between devices with their start and end apart: 1 -> 0, of which waited for: 1 -> 0; matrix products, arithmetic and copies ran while one was open for 19% -> 0% of each run, Pallas kernels for 0% -> 0%
where the time goes in v1:
time: 135 us; the launch traced here: 134 us
  Pallas kernels  117 us (87%)
  local copies, waits for them, and re-layouts  8.91 us (7%)
  other arithmetic  8.13 us (6%)
    pallas_call x1, Pallas kernels, shards(): pl.pallas_call(functools.partial(exchange_kernel, groups, sizes), out_sha...  117 us
    select_n x1, other arithmetic, shards(): attention = jnp.where(live[:, :, None], attended, 0.0).astype(jnp.bfloat16)  2.72 us

profile of v1, /device:TPU:0, one launch (start us, length us, event | category | flops | bytes accessed | tf_op | source)
XLA Modules:
  0.0 134.3 jit_solution(5898108880952753821)
XLA Ops:
  0.6 0.8 compare_convert_fusion
  1.4 0.7 iota_compare_fusion.1
  2.1 0.1 add_convert_fusion
  2.2 0.1 convert_element_type.17
  2.3 1.3 reshape.105.gain_ref
  3.6 2.0 %fusion = (s32[32,2]{1,0:T(8,128)S(1)}, s32[32,2]{1,0:T(8,128)S(1)}) fusion(s32[32,32,2]{1,2,0:T(2,128)} %param.25, s32[]{:T(128)S(6)} %select_n.39, s32[32,32,2]{1,2,0:T(2,128)} %param.24), kind=kLoop, calls=%fused_computation.6 | loop fusion | flops 128 | bytes 1028 | tf_op jit(solution)/shard_map/jit(_where)/select_n | solution.py:419
  5.7 0.1 select_n.41
  5.8 0.1 eq.28
  5.9 0.1 select_reduce_fusion
  6.0 0.6 pad_add_fusion.slot_ref
  6.6 0.3 fusion.1
  7.0 0.8 pad_maximum_fusion
  7.7 1.0 copy.20
  8.7 0.9 reshape.103.row_ref
  9.6 1.0 copy.21
  10.6 0.9 reshape.104.seq_ref
  11.5 116.5 %page_exchange.1 = (bf16[32,128,128]{2,1,0:T(8,128)(2,1)}, bf16[128,1024]{1,0:T(8,128)(2,1)}, bf16[128,1024]{1,0:T(8,128)(2,1)}) custom-call(s32[2048]{0:T(1024)} %reshape.103.row_ref, s32[2048]{0:T(1024)} %reshape.104.seq_ref, s32[1024]{0:T(1024)} %len_ref.1, s32[96]{0:T(128)} %pad_add_fusion.slot_ref, bf16[32,4,5120]{2,1,0:T(4,128)(2,1)} %x_ref, ...), custom_call_target="tpu_custom_call" | custom-call | tf_op jit(solution)/shard_map/page_exchange/pallas_call | solution.py:435
  128.0 2.7 %broadcast_select_fusion = bf16[32,4,4096]{2,1,0:T(4,128)(2,1)} fusion(bf16[32,4,4096]{2,1,0:T(4,128)(2,1)} %bitcast.11, pred[32,4]{1,0:T(8,128)(4,1)S(1)} %iota_compare_fusion.1), kind=kLoop, calls=%fused_computation | loop fusion | flops 524288 | bytes 2097280 | tf_op jit(solution)/shard_map/jit(_where)/select_n | solution.py:491
  130.8 1.8 %reshape.112 = bf16[32,4,1024]{2,1,0:T(4,128)(2,1)} reshape(bf16[128,1024]{1,0:T(8,128)(2,1)} %get-tuple-element.7) | data formatting | bytes 524288 | tf_op jit(solution)/shard_map/reshape | solution.py:494
  132.5 1.8 %reshape.113 = bf16[32,4,1024]{2,1,0:T(4,128)(2,1)} reshape(bf16[128,1024]{1,0:T(8,128)(2,1)} %get-tuple-element.8) | data formatting | bytes 524288 | tf_op jit(solution)/shard_map/reshape | solution.py:495
  (3 shorter events, 0.0 us)

commit v2 on v1

--- a/solution.py
+++ b/solution.py
@@ -11,31 +11,32 @@
 EPSILON = 1e-06
 ROPE_BASE = 1000000.0
 MASKED_SCORE = -1e30
-DEPTH = 4
+DEPTH = 6
+PAIR = 2
 WEIGHT_BUFFERS = 3
 
 
 def soft_parts(scores, mask, head_width):
     scores = jnp.where(mask, scores * (1.0 / math.sqrt(head_width)), MASKED_SCORE)
-    top = jnp.max(scores, axis=0, keepdims=True)
-    weights = jnp.where(mask, jnp.exp(scores - top), 0.0)
-    weights = weights.astype(jnp.bfloat16).astype(jnp.float32)
+    top = jnp.maximum(jnp.max(scores, axis=0, keepdims=True), 0.1 * MASKED_SCORE)
+    weights = jnp.exp(scores - top).astype(jnp.bfloat16).astype(jnp.float32)
     return top, jnp.sum(weights, axis=0, keepdims=True), weights.T.astype(jnp.bfloat16)
 
 
-def spread_dot(keys, block_q):
-    return lax.dot_general(
-        keys, block_q, (((1,), (1,)), ((), ())), preferred_element_type=jnp.float32
+def spread_dot(keys, queries, heads, per_head):
+    turned = queries.astype(jnp.float32).T.astype(jnp.bfloat16)
+    head_of = lax.broadcasted_iota(jnp.int32, turned.shape, 1) // per_head
+    spread = [jnp.where(head_of == h, turned, jnp.zeros_like(turned)) for h in range(heads)]
+    return jnp.dot(
+        keys, jnp.concatenate(spread, axis=0), preferred_element_type=jnp.float32
     )
 
 
 def exchange_kernel(
     n,
     sizes,
-    row_ref,
-    seq_ref,
+    table_ref,
     len_ref,
-    slot_ref,
     x_ref,
     gain_ref,
     cos_ref,
@@ -61,7 +62,6 @@
     s_recv,
     kbuf,
     vbuf,
-    block_q,
     new_o,
     new_s,
     q_ssem,
@@ -94,14 +94,16 @@
     def before(k):
         return lax.rem(me + n - distance(k), n)
 
+    count = n * cap
+
     def own_row(holder, c):
-        return jnp.minimum(row_ref[(holder * n + me) * cap + c], rows - 1)
+        return table_ref[holder * cap + c]
 
     def usable_tokens(owner, c):
-        index = (me * n + owner) * cap + c
-        row = row_ref[index]
+        index = count + owner * cap + c
+        row = table_ref[index]
         length = len_ref[owner * rows + jnp.minimum(row, rows - 1)]
-        return jnp.where(row < rows, length, 0) - seq_ref[index] * page
+        return jnp.where(row < rows, length, 0) - table_ref[index + count] * page
 
     def fetch(k):
         owner, buf = before(k), lax.rem(k, depth)
@@ -196,7 +198,7 @@
 
     for j in range(bufs - 1):
         weight(jnp.int32(j), start)
-    for k in range(depth - 1):
+    for k in range(depth - PAIR):
         for copy in fetch(k):
             copy.start()
 
@@ -208,7 +210,6 @@
             barrier, inc=1, device_id={"dp": after(k)}, device_id_type=pl.DeviceIdType.MESH
         )
 
-    block_q[...] = jnp.zeros_like(block_q)
     x = x_ref[...].astype(jnp.float32).reshape(normed.shape)
     scale = lax.rsqrt(jnp.mean(x * x, axis=-1, keepdims=True) + EPSILON)
     normed[...] = (x * scale * gain_ref[...].astype(jnp.float32)).astype(jnp.bfloat16)
@@ -255,49 +256,57 @@
     def stripe(h):
         return slice(h * per_head, (h + 1) * per_head)
 
-    @pl.loop(0, n)
-    def _(k):
-        owner, buf = before(k), lax.rem(k, depth)
-
-        @pl.when(k + depth - 1 < n)
-        def _():
-            for copy in fetch(k + depth - 1):
-                copy.start()
-
-        @pl.when(k > 0)
-        def _():
-            for part in range(parts):
-                recv_query(part, k).wait_recv()
-
-        for copy in fetch(k):
-            copy.wait()
-        scores = []
-        for c in range(cap):
-            for h in range(heads):
-                part, first = h // part_heads, (h % part_heads) * per_head
-                block_q[c, stripe(h), columns(h)] = q_recv[
-                    part, owner, c, first : first + per_head
-                ]
-            scores.append(spread_dot(kbuf[buf, c], block_q[c]))
+    @pl.loop(0, n // PAIR)
+    def _(turn):
+        ks = [turn * PAIR + i for i in range(PAIR)]
+        for k in ks:
+
+            @pl.when(k + depth - PAIR < n)
+            def _():
+                for copy in fetch(k + depth - PAIR):
+                    copy.start()
+
+        for k in ks:
+
+            @pl.when(k > 0)
+            def _():
+                for part in range(parts):
+                    recv_query(part, k).wait_recv()
+
+            for copy in fetch(k):
+                copy.wait()
+
+        slots = [(before(k), lax.rem(k, depth), c) for k in ks for c in range(cap)]
+        scores = [
+            spread_dot(
+                kbuf[buf, c],
+                jnp.concatenate([q_recv[part, owner, c] for part in range(parts)], axis=0),
+                heads,
+                per_head,
+            )
+            for owner, buf, c in slots
+        ]
         turned = []
-        for c in range(cap):
+        for (owner, buf, c), found in zip(slots, scores):
             mask = position < usable_tokens(owner, c)
-            top, total, weights = soft_parts(scores[c], mask, head_width)
+            top, total, weights = soft_parts(found, mask, head_width)
             s_send[owner, 2 * c : 2 * c + 1, 0:width] = top
             s_send[owner, 2 * c + 1 : 2 * c + 2, 0:width] = total
             turned.append(weights)
-        for c in range(cap):
+        for (owner, buf, c), weights in zip(slots, turned):
             for h in range(heads):
                 o_send[owner, c, stripe(h)] = jnp.dot(
-                    turned[c][stripe(h)],
+                    weights[stripe(h)],
                     vbuf[buf, c, :, columns(h)],
                     preferred_element_type=jnp.float32,
                 ).astype(jnp.bfloat16)
 
-        @pl.when(k > 0)
-        def _():
-            for copy in send_back(owner, me):
-                copy.start()
+        for k in ks:
+
+            @pl.when(k > 0)
+            def _():
+                for copy in send_back(before(k), me):
+                    copy.start()
 
     per_tile = 16 // steps
     token = lax.broadcasted_iota(jnp.int32, (16, width), 0)
@@ -310,9 +319,7 @@
         keys, values = nk_ref[at], nv_ref[at]
         scores = []
         for i in range(per_tile):
-            for h in range(heads):
-                block_q[i, stripe(h), columns(h)] = q_own[tile * per_tile + i, stripe(h)]
-            scores.append(spread_dot(keys, block_q[i]))
+            scores.append(spread_dot(keys, q_own[tile * per_tile + i], heads, per_head))
         turned = []
         for i in range(per_tile):
             row = tile * per_tile + i
@@ -340,8 +347,8 @@
 
     @pl.loop(0, rows, unroll=2)
     def _(r):
-        first, second = slot_ref[r], slot_ref[rows + r]
-        has_second = slot_ref[2 * rows + r]
+        first, second = table_ref[3 * count + r], table_ref[3 * count + rows + r]
+        has_second = table_ref[3 * count + 2 * rows + r]
 
         def stats(slot):
             both = s_recv[slot // cap]
@@ -420,7 +427,11 @@
     both = jnp.sum(jnp.where(holds, shifted, 0), axis=1)
     slot_a, slot_b = both % slot_count, both // slot_count
     has_b = (local_lengths > page_len).astype(jnp.int32)
-    slots = jnp.concatenate([slot_a, slot_b, has_b])
+    held_rows = lax.dynamic_index_in_dim(page_row, my_group, 0, keepdims=False).reshape(-1)
+    held_seq = lax.dynamic_index_in_dim(page_seq, my_group, 0, keepdims=False).reshape(-1)
+    table = jnp.concatenate(
+        [jnp.minimum(sent_rows, row_count - 1), held_rows, held_seq, slot_a, slot_b, has_b]
+    )
     width = kv_heads * per_head
     lanes = max(128, width)
     sizes = (row_count, kv_heads, per_head, head_width, step_count, capacity, page_len)
@@ -439,7 +450,7 @@
             jax.ShapeDtypeStruct((tokens, features), bf16),
             jax.ShapeDtypeStruct((tokens, features), bf16),
         ),
-        in_specs=[smem] * 4 + [vmem] * 6 + [hbm] * 5,
+        in_specs=[smem] * 2 + [vmem] * 6 + [hbm] * 5,
         out_specs=(vmem, vmem, vmem),
         scratch_shapes=[
             pltpu.VMEM((tokens, feature_count), bf16),
@@ -453,7 +464,6 @@
             pltpu.VMEM((groups, 2 * capacity, lanes), f32),
             pltpu.VMEM((DEPTH, capacity, page_len, features), bf16),
             pltpu.VMEM((DEPTH, capacity, page_len, features), bf16),
-            pltpu.VMEM((max(capacity, 16 // step_count), width, features), bf16),
             pltpu.VMEM((row_count, width, head_width), f32),
             pltpu.VMEM((row_count, 2, lanes), f32),
         ]
@@ -466,10 +476,8 @@
         ),
         name="page_exchange",
     )(
-        page_row.reshape(-1),
-        page_seq.reshape(-1),
+        table,
         cache_len,
-        slots,
         gathered,
         full_gain.reshape(1, feature_count),
         cosine,

time: 135 us -> 133 us (0.985)
  local copies, waits for them, and re-layouts: 8.91 us -> 6.88 us
    unnamed x2 -> x0, local copies, waits for them, and re-layouts: 2.04 us -> none
    reshape x2 -> x3, local copies, waits for them, and re-layouts: 1.73 us -> 0.31 us  [the longest x1 0.11 us: shards(): lax.dynamic_index_in_dim(page_row, my_group, 0, keepdims=False).reshape(-1)]
where the time goes in v2:
time: 133 us; the launch traced here: 132 us
  Pallas kernels  117 us (88%)
  other arithmetic  7.51 us (6%)
  local copies, waits for them, and re-layouts  6.88 us (5%)
    pallas_call x1, Pallas kernels, shards(): pl.pallas_call(functools.partial(exchange_kernel, groups, sizes), out_sha...  117 us
    select_n x1, other arithmetic, shards(): attention = jnp.where(live[:, :, None], attended, 0.0).astype(jnp.bfloat16)  2.72 us

profile of v2, /device:TPU:0, one launch (start us, length us, event | category | flops | bytes accessed | tf_op | source)
XLA Modules:
  0.0 131.7 jit_solution(6037579262163686475)
XLA Ops:
  0.6 0.8 compare_convert_fusion
  1.4 0.7 constant_dynamic-slice_fusion
  2.1 0.7 iota_compare_fusion.1
  2.8 0.1 copy.23
  2.9 0.1 reshape.111
  3.0 0.1 copy.22
  3.1 0.1 reshape.110
  3.2 0.1 add_convert_fusion
  3.3 0.1 convert_element_type.17
  3.4 1.3 %reshape.112.gain_ref = bf16[1,5120]{1,0:T(2,128)(2,1)} reshape(bf16[5120]{0:T(1024)(128)(2,1)} %param.14) | data formatting | bytes 20480 | tf_op jit(solution)/shard_map/reshape | solution.py:482
  4.7 2.0 %fusion = (s32[32,2]{1,0:T(8,128)S(1)}, s32[32,2]{1,0:T(8,128)S(1)}) fusion(s32[32,32,2]{1,2,0:T(2,128)} %param.25, s32[]{:T(128)S(6)} %select_n.42, s32[32,32,2]{1,2,0:T(2,128)} %param.24), kind=kLoop, calls=%fused_computation.6 | loop fusion | flops 128 | bytes 1028 | tf_op jit(solution)/shard_map/jit(_where)/select_n | solution.py:426
  6.8 0.1 select_n.44
  6.9 0.1 reshape.109
  7.0 0.1 select_reduce_fusion
  7.1 0.7 concatenate.9.table_ref
  7.8 0.3 fusion.1
  8.1 0.8 pad_maximum_fusion
  8.9 116.6 %page_exchange.1 = (bf16[32,128,128]{2,1,0:T(8,128)(2,1)}, bf16[128,1024]{1,0:T(8,128)(2,1)}, bf16[128,1024]{1,0:T(8,128)(2,1)}) custom-call(s32[288]{0:T(512)} %concatenate.9.table_ref, s32[1024]{0:T(1024)} %len_ref.1, bf16[32,4,5120]{2,1,0:T(4,128)(2,1)} %x_ref, bf16[1,5120]{1,0:T(2,128)(2,1)} %reshape.112.gain_ref, f32[128,128]{1,0:T(8,128)} %get-tuple-element.20.cos_ref, ...), custom_call_target="tpu_custom_call" | custom-call | tf_op jit(solution)/shard_map/page_exchange/pallas_call | solution.py:446
  125.5 2.7 %broadcast_select_fusion = bf16[32,4,4096]{2,1,0:T(4,128)(2,1)} fusion(bf16[32,4,4096]{2,1,0:T(4,128)(2,1)} %bitcast.11, pred[32,4]{1,0:T(8,128)(4,1)S(1)} %iota_compare_fusion.1), kind=kLoop, calls=%fused_computation | loop fusion | flops 524288 | bytes 2097280 | tf_op jit(solution)/shard_map/jit(_where)/select_n | solution.py:499
  128.2 1.8 %reshape.119 = bf16[32,4,1024]{2,1,0:T(4,128)(2,1)} reshape(bf16[128,1024]{1,0:T(8,128)(2,1)} %get-tuple-element.7) | data formatting | bytes 524288 | tf_op jit(solution)/shard_map/reshape | solution.py:502
  130.0 1.8 %reshape.120 = bf16[32,4,1024]{2,1,0:T(4,128)(2,1)} reshape(bf16[128,1024]{1,0:T(8,128)(2,1)} %get-tuple-element.8) | data formatting | bytes 524288 | tf_op jit(solution)/shard_map/reshape | solution.py:503
  (4 shorter events, 0.0 us)

commit v3 on v2

--- a/solution.py
+++ b/solution.py
@@ -49,9 +49,11 @@
     ck_ref,
     cv_ref,
     out_ref,
+    keys_ref,
+    values_ref,
+    normed,
     nk_ref,
     nv_ref,
-    normed,
     wbuf,
     q_own,
     q_send,
@@ -77,6 +79,7 @@
     rows, heads, per_head, head_width, steps, cap, page, depth, parts = sizes
     width = heads * per_head
     part_heads = heads // parts
+    group = 2 if heads % 2 == 0 else 1
     part_rows = part_heads * per_head
     block_cols = wbuf.shape[2]
     key_cols = min(block_cols, wk_ref.shape[1])
@@ -86,7 +89,10 @@
     me = lax.axis_index("dp")
 
     def distance(k):
-        return k // 2 + (n // 2) * lax.rem(k, 2)
+        far_first = k // 2 + (n // 2) * lax.rem(k, 2)
+        near_first = (k + 1) // 2 + (n // 2 - 1) * (1 - lax.rem(k, 2))
+        ends = (k == 0) | (k == n - 1)
+        return jnp.where((lax.rem(me, 2) == 0) | ends, far_first, near_first)
 
     def after(k):
         return lax.rem(me + distance(k), n)
@@ -241,12 +247,16 @@
     def _(j):
         done = rotated(project(j + heads, key_cols), k_gain_ref[...].astype(jnp.float32))
         at = pl.ds(pl.multiple_of(j * key_cols, key_cols), key_cols)
-        nk_ref[:, at] = jnp.concatenate(done, axis=1).astype(jnp.bfloat16)
+        made = jnp.concatenate(done, axis=1)
+        nk_ref[:, at] = made.astype(jnp.bfloat16)
+        keys_ref[:, :, at] = made.reshape(rows, steps, key_cols).astype(jnp.bfloat16)
 
     @pl.loop(0, key_blocks)
     def _(j):
         at = pl.ds(pl.multiple_of(j * key_cols, key_cols), key_cols)
-        nv_ref[:, at] = project(j + heads + key_blocks, key_cols).astype(jnp.bfloat16)
+        made = project(j + heads + key_blocks, key_cols)
+        nv_ref[:, at] = made.astype(jnp.bfloat16)
+        values_ref[:, :, at] = made.reshape(rows, steps, key_cols).astype(jnp.bfloat16)
 
     position = lax.broadcasted_iota(jnp.int32, (page, width), 0)
 
@@ -293,13 +303,31 @@
             s_send[owner, 2 * c : 2 * c + 1, 0:width] = top
             s_send[owner, 2 * c + 1 : 2 * c + 2, 0:width] = total
             turned.append(weights)
-        for (owner, buf, c), weights in zip(slots, turned):
-            for h in range(heads):
-                o_send[owner, c, stripe(h)] = jnp.dot(
-                    weights[stripe(h)],
-                    vbuf[buf, c, :, columns(h)],
+        for i in range(PAIR):
+            owner, buf, _ = slots[i * cap]
+            values = vbuf[buf].reshape(cap * page, heads * head_width)
+            for h in range(0, heads, group):
+                left = [
+                    jnp.concatenate(
+                        [
+                            taken if c == other else jnp.zeros_like(taken)
+                            for other in range(cap)
+                        ],
+                        axis=1,
+                    )
+                    for c, taken in enumerate(
+                        turned[i * cap + c][h * per_head : (h + group) * per_head]
+                        for c in range(cap)
+                    )
+                ]
+                outs = jnp.dot(
+                    jnp.concatenate(left, axis=0),
+                    values[:, h * head_width : (h + group) * head_width],
                     preferred_element_type=jnp.float32,
                 ).astype(jnp.bfloat16)
+                for c in range(cap):
+                    for j in range(group):
+                        o_send[owner, c, stripe(h + j)] = outs[stripe(c * group + j), columns(j)]
 
         for k in ks:
 
@@ -345,35 +373,43 @@
         for copy in send_back(after(k), after(k)):
             copy.wait_recv()
 
-    @pl.loop(0, rows, unroll=2)
-    def _(r):
-        first, second = table_ref[3 * count + r], table_ref[3 * count + rows + r]
-        has_second = table_ref[3 * count + 2 * rows + r]
-
-        def stats(slot):
-            both = s_recv[slot // cap]
-            top, total = both[0:1], both[1:2]
-            for c in range(1, cap):
-                hit = lax.rem(slot, cap) == c
-                top = jnp.where(hit, both[2 * c : 2 * c + 1], top)
-                total = jnp.where(hit, both[2 * c + 1 : 2 * c + 2], total)
-            return top, total
-
+    def row_slots(r):
+        at = 3 * count + r
+        return table_ref[at], table_ref[at + rows], table_ref[at + 2 * rows]
+
+    def stats(slot):
+        both = s_recv[slot // cap]
+        top, total = both[0:1], both[1:2]
+        for c in range(1, cap):
+            hit = lax.rem(slot, cap) == c
+            top = jnp.where(hit, both[2 * c : 2 * c + 1], top)
+            total = jnp.where(hit, both[2 * c + 1 : 2 * c + 2], total)
+        return top, total
+
+    shares = []
+    for r in range(rows):
+        first, second, has_second = row_slots(r)
         top_a, total_a = stats(first)
         top_b, total_b = stats(second)
         top_b = jnp.where(has_second > 0, top_b, MASKED_SCORE)
-        total_b = jnp.where(has_second > 0, total_b, 0.0)
         top_n, total_n = new_s[r, 0:1], new_s[r, 1:2]
         top = jnp.maximum(jnp.maximum(top_a, top_b), top_n)
         fa, fb, fn = jnp.exp(top_a - top), jnp.exp(top_b - top), jnp.exp(top_n - top)
         fb = jnp.where(has_second > 0, fb, 0.0)
         share = 1.0 / (fa * total_a + fb * total_b + fn * total_n)
-        factors = jnp.concatenate(
-            [fa * share, fb * share, fn * share, jnp.zeros((5, fa.shape[1]), jnp.float32)], axis=0
-        ).T[0:width]
+        shares += [fa * share, fb * share, fn * share]
+    fill = -len(shares) % 128
+    shares.append(jnp.zeros((fill, shares[0].shape[1]), jnp.float32))
+    factors = jnp.concatenate(shares, axis=0).T[0:width]
+    for r in range(rows):
+        first, second, _ = row_slots(r)
         out_a = o_recv[first // cap, lax.rem(first, cap)].astype(jnp.float32)
         out_b = o_recv[second // cap, lax.rem(second, cap)].astype(jnp.float32)
-        out = factors[:, 0:1] * out_a + factors[:, 1:2] * out_b + factors[:, 2:3] * new_o[r]
+        out = (
+            factors[:, 3 * r : 3 * r + 1] * out_a
+            + factors[:, 3 * r + 1 : 3 * r + 2] * out_b
+            + factors[:, 3 * r + 2 : 3 * r + 3] * new_o[r]
+        )
         out_ref[r] = out.astype(out_ref.dtype)
 
 
@@ -435,7 +471,7 @@
     width = kv_heads * per_head
     lanes = max(128, width)
     sizes = (row_count, kv_heads, per_head, head_width, step_count, capacity, page_len)
-    parts = 2 if kv_heads % 2 == 0 else 1
+    parts = math.gcd(4, kv_heads)
     sizes = sizes + (DEPTH, parts)
     smem = pl.BlockSpec(memory_space=pltpu.SMEM)
     vmem = pl.BlockSpec(memory_space=pltpu.VMEM)
@@ -447,13 +483,15 @@
         functools.partial(exchange_kernel, groups, sizes),
         out_shape=(
             jax.ShapeDtypeStruct((row_count, width, head_width), bf16),
-            jax.ShapeDtypeStruct((tokens, features), bf16),
-            jax.ShapeDtypeStruct((tokens, features), bf16),
+            jax.ShapeDtypeStruct((row_count, step_count, features), bf16),
+            jax.ShapeDtypeStruct((row_count, step_count, features), bf16),
         ),
         in_specs=[smem] * 2 + [vmem] * 6 + [hbm] * 5,
         out_specs=(vmem, vmem, vmem),
         scratch_shapes=[
             pltpu.VMEM((tokens, feature_count), bf16),
+            pltpu.VMEM((tokens, features), bf16),
+            pltpu.VMEM((tokens, features), bf16),
             pltpu.VMEM((WEIGHT_BUFFERS, feature_count, group_size * head_width), bf16),
             pltpu.VMEM((row_count, width, head_width), bf16),
             pltpu.VMEM((parts, groups, capacity, width // parts, head_width), bf16),

time: 133 us -> 126 us (0.947)
  Pallas kernels: 117 us -> 109 us
    pallas_call x1, Pallas kernels: 117 us -> 109 us  [shards(): pl.pallas_call(functools.partial(exchange_kernel, groups, sizes), out_sha...]
    reshape x2 -> x0, local copies, waits for them, and re-layouts: 3.51 us -> none  [the longest x1 1.76 us: shards(): fresh_keys.reshape(row_count, step_count, -1)]
    unnamed x0 -> x2, local copies, waits for them, and re-layouts: none -> 3.49 us
where the time goes in v3:
time: 126 us; the launch traced here: 124 us
  Pallas kernels  109 us (87%)
  other arithmetic  7.51 us (6%)
  local copies, waits for them, and re-layouts  6.86 us (5%)
    pallas_call x1, Pallas kernels, shards(): pl.pallas_call(functools.partial(exchange_kernel, groups, sizes), out_sha...  109 us
    unnamed x2, local copies, waits for them, and re-layouts  3.49 us
    select_n x1, other arithmetic, shards(): attention = jnp.where(live[:, :, None], attended, 0.0).astype(jnp.bfloat16)  2.72 us

profile of v3, /device:TPU:0, one launch (start us, length us, event | category | flops | bytes accessed | tf_op | source)
XLA Modules:
  0.0 123.9 jit_solution(5266253134263998789)
XLA Ops:
  0.6 0.8 compare_convert_fusion
  1.4 0.7 constant_dynamic-slice_fusion
  2.1 0.7 iota_compare_fusion.1
  2.8 0.1 copy.23
  2.9 0.1 reshape.105
  3.0 0.1 copy.22
  3.1 0.1 reshape.104
  3.2 0.1 add_convert_fusion
  3.3 0.1 convert_element_type.17
  3.4 1.3 %reshape.106.gain_ref = bf16[1,5120]{1,0:T(2,128)(2,1)} reshape(bf16[5120]{0:T(1024)(128)(2,1)} %param.14) | data formatting | bytes 20480 | tf_op jit(solution)/shard_map/reshape | solution.py:520
  4.7 2.0 %fusion = (s32[32,2]{1,0:T(8,128)S(1)}, s32[32,2]{1,0:T(8,128)S(1)}) fusion(s32[32,32,2]{1,2,0:T(2,128)} %param.25, s32[]{:T(128)S(6)} %select_n.42, s32[32,32,2]{1,2,0:T(2,128)} %param.24), kind=kLoop, calls=%fused_computation.6 | loop fusion | flops 128 | bytes 1028 | tf_op jit(solution)/shard_map/jit(_where)/select_n | solution.py:462
  6.8 0.1 select_n.44
  6.9 0.1 reshape.103
  7.0 0.1 select_reduce_fusion
  7.1 0.7 concatenate.9.table_ref
  7.8 0.3 fusion.1
  8.1 0.8 pad_maximum_fusion
  8.9 108.8 %page_exchange.1 = (bf16[32,128,128]{2,1,0:T(8,128)(2,1)}, bf16[32,4,1024]{2,1,0:T(4,128)(2,1)}, bf16[32,4,1024]{2,1,0:T(4,128)(2,1)}) custom-call(s32[288]{0:T(512)} %concatenate.9.table_ref, s32[1024]{0:T(1024)} %len_ref.1, bf16[32,4,5120]{2,1,0:T(4,128)(2,1)} %x_ref, bf16[1,5120]{1,0:T(2,128)(2,1)} %reshape.106.gain_ref, ...), custom_call_target="tpu_custom_call" | custom-call | tf_op jit(solution)/shard_map/page_exchange/pallas_call | solution.py:482
  117.7 2.7 %broadcast_select_fusion = bf16[32,4,4096]{2,1,0:T(4,128)(2,1)} fusion(bf16[32,4,4096]{2,1,0:T(4,128)(2,1)} %bitcast.11, pred[32,4]{1,0:T(8,128)(4,1)S(1)} %iota_compare_fusion.1), kind=kLoop, calls=%fused_computation | loop fusion | flops 524288 | bytes 2097280 | tf_op jit(solution)/shard_map/jit(_where)/select_n | solution.py:537
  120.4 1.7 %copy.27 = bf16[32,4,1024]{2,1,0:T(4,128)(2,1)} copy(bf16[32,4,1024]{2,1,0:T(4,128)(2,1)} %get-tuple-element.26) | data formatting | bytes 524288
  122.1 1.7 %copy.28 = bf16[32,4,1024]{2,1,0:T(4,128)(2,1)} copy(bf16[32,4,1024]{2,1,0:T(4,128)(2,1)} %get-tuple-element.27) | data formatting | bytes 524288
  (4 shorter events, 0.0 us)
